TPU v7x, 512 devices: a whole 4x4x16 slice. The times are simulated.
512 devices in a mesh: chan: 32 (over z, y_hi), freq: 16 (over y_lo, x, core).
Axes of the slice: x: 4, y: 4 (y_hi: 2, y_lo: 2; y = y_hi * 2 + y_lo), z: 16, core: 2. Of those that a mesh axis runs over, the one named last changes fastest.
Arguments:
- signal: bfloat16 [4096, 131072], P('chan', 'freq'), may hold values from -6 to 6
Outputs:
- cross_spectra: bfloat16 [2, 1024, 32, 4096], P(None, 'freq', None, 'chan')
All inputs are finite; a program needn't handle non-finite values.
Results may differ from a plain program's by a relative error of at most 0.01.
Values may be sent and summed in bfloat16 or wider, within the bound.
A program may use at most 64 MiB of HBM per device.

v0:
```python
import math

import jax
import jax.numpy as jnp
from jax import lax
from jax.sharding import PartitionSpec as P

L = 2048
SEG_DEV = 4
REF_DEV = 1
BINS = 1024


def make_table(groups):
    per_group = BINS // groups
    n = jnp.arange(L, dtype=jnp.int32)[:, None]
    column = jnp.arange(2 * BINS, dtype=jnp.int32)[None, :]
    group = column // (2 * per_group)
    within = column % (2 * per_group)
    second = within // per_group
    k = group * per_group + within % per_group
    angle = 2.0 * math.pi * (n * k % L).astype(jnp.float32) / L
    values = jnp.where(second == 0, jnp.cos(angle), -jnp.sin(angle))
    return values.astype(jnp.bfloat16)


def local(signal):
    groups = lax.axis_size("freq")
    rows = signal.shape[0]
    n = jnp.arange(L, dtype=jnp.float32)
    window = 0.5 - 0.5 * jnp.cos(2.0 * math.pi * n / L)
    power = jnp.sum(window * window)
    seg = signal.astype(jnp.float32).reshape(rows, SEG_DEV, L)
    seg = seg - jnp.mean(seg, axis=2, keepdims=True)
    windowed = (seg * window).astype(jnp.bfloat16)
    table = make_table(groups)
    spectra = jnp.dot(
        windowed.reshape(rows * SEG_DEV, L), table, preferred_element_type=jnp.float32
    )
    spectra = spectra.astype(jnp.bfloat16).reshape(rows, SEG_DEV, 2 * BINS)
    local_spec = lax.all_to_all(spectra, "freq", split_axis=2, concat_axis=1, tiled=True)
    ref_spec = lax.all_gather(local_spec[:REF_DEV], "chan", axis=0, tiled=True)
    per_group = local_spec.shape[2] // 2
    chan_re = local_spec[:, :, :per_group]
    chan_im = local_spec[:, :, per_group:]
    ref_re = ref_spec[:, :, :per_group]
    ref_im = ref_spec[:, :, per_group:]
    real_part = jnp.einsum("csk,rsk->krc", chan_re, ref_re, preferred_element_type=jnp.float32)
    real_part = real_part + jnp.einsum(
        "csk,rsk->krc", chan_im, ref_im, preferred_element_type=jnp.float32
    )
    imag_part = jnp.einsum("csk,rsk->krc", chan_im, ref_re, preferred_element_type=jnp.float32)
    imag_part = imag_part - jnp.einsum(
        "csk,rsk->krc", chan_re, ref_im, preferred_element_type=jnp.float32
    )
    total_segs = local_spec.shape[1]
    scale = 1.0 / (total_segs * power)
    return (jnp.stack([real_part, imag_part]) * scale).astype(jnp.bfloat16)


def solution(mesh):
    in_specs = (P("chan", "freq"),)
    out_specs = P(None, "freq", None, "chan")
    return jax.shard_map(local, mesh=mesh, in_specs=in_specs, out_specs=out_specs, check_vma=False)
```

profile of v0, /device:TPU:6, one launch (start us, length us, event | category | flops | bytes accessed | tf_op | source)
XLA Modules:
  0.0 228.2 jit_solution(13503073383692462825)
XLA Ops:
  0.0 0.0 copy-start.1
  0.0 6.2 %reshape.136 = f32[128,4,2048]{2,1,0:T(4,128)} reshape(bf16[128,8192]{1,0:T(8,128)(2,1)} %param.1) | data formatting | bytes 6291456 | tf_op jit(solution)/shard_map/reshape | solution.py:33
  6.2 0.0 copy-done.1
  6.2 3.0 %reshape.135 = f32[512,2048]{1,0:T(8,128)} reshape(bf16[128,8192]{1,0:T(8,128)(2,1)S(1)} %copy-done.1) | data formatting | bytes 6291456 | tf_op jit(solution)/shard_map/reshape | solution.py:33
  9.2 0.1 multiply_subtract_fusion
  9.3 2.8 %reduce_sum.18 = f32[128,4]{1,0:T(8,128)S(1)} reduce(f32[128,4,2048]{2,1,0:T(4,128)} %reshape.136, f32[]{:T(128)} %constant.71.clone.1), dimensions={2}, to_apply=%region_0.0 | reduce | flops 1048064 | bytes 4196356 | tf_op jit(solution)/shard_map/reduce_sum | solution.py:34
  12.1 0.1 div.45
  12.2 2.6 %multiply_convert_fusion.5 = bf16[512,2048]{1,0:T(8,128)(2,1)S(1)} fusion(f32[512,2048]{1,0:T(8,128)} %reshape.135, f32[2048]{0:T(1024)S(1)} %multiply_subtract_fusion, f32[512]{0:T(512)S(1)} %div.45), kind=kLoop, calls=%fused_computation.17.clone.clone.2 | loop fusion | flops 3145728 | bytes 6301696 | tf_op jit(solution)/shard_map/dot_general | solution.py:37
  14.8 70.3 %fusion.13 = bf16[512,2048]{1,0:T(8,128)(2,1)} fusion(s32[2048]{0:T(1024)S(1)} %fusion.28, pred[2048]{0:T(1024)(128)(4,1)S(1)} %fusion.25, bf16[512,2048]{1,0:T(8,128)(2,1)S(1)} %multiply_convert_fusion.5), kind=kOutput, calls=%fused_computation.18 | convolution fusion | flops 4367319040 | bytes 4204544 | tf_op jit(solution)/shard_map/dot_general | solution.py:37
  85.1 2.7 %reshape.137 = bf16[128,4,2048]{2,1,0:T(4,128)(2,1)S(1)} reshape(bf16[512,2048]{1,0:T(8,128)(2,1)} %fusion.13) | data formatting | bytes 4194304 | tf_op jit(solution)/shard_map/reshape | solution.py:40
  87.9 3.7 %copy.10 = bf16[128,4,2048]{0,1,2:T(4,128)(2,1)} copy(bf16[128,4,2048]{2,1,0:T(4,128)(2,1)S(1)} %reshape.137) | data formatting | bytes 4194304 | tf_op jit(solution)/shard_map/reshape | solution.py:40
  91.5 9.4 %all-to-all-start = ((bf16[128,4,2048]{0,1,2:T(4,128)(2,1)}), bf16[128,4,2048]{0,1,2:T(4,128)(2,1)S(1)}, u32[]{:S(2)}, u32[]{:S(2)}) async-start(bf16[128,4,2048]{0,1,2:T(4,128)(2,1)} %copy.10), calls=%async_computation | async-start | bytes 4194304 | tf_op jit(solution)/shard_map/all_to_all | solution.py:41
  100.9 0.7 multiply_reduce_fusion
  102.3 24.3 %all-to-all-done = bf16[128,4,2048]{0,1,2:T(4,128)(2,1)S(1)} async-done(((bf16[128,4,2048]{0,1,2:T(4,128)(2,1)}), bf16[128,4,2048]{0,1,2:T(4,128)(2,1)S(1)}, u32[]{:S(2)}, u32[]{:S(2)}) %all-to-all-start) | async-done | bytes 2097184 | tf_op jit(solution)/shard_map/all_to_all | solution.py:41
  126.6 0.0 copy-start
  126.6 1.3 copy-done
  128.0 2.8 %copy.13 = bf16[128,16,4,128]{0,2,1,3:T(4,128)(2,1)S(1)} copy(bf16[128,16,4,128]{0,2,3,1:T(4,128)(2,1)} %bitcast.19) | data formatting | bytes 4194304 | tf_op jit(solution)/shard_map/all_to_all | solution.py:41
  130.7 5.5 %copy.11 = bf16[128,4,16,128]{3,1,2,0:T(4,128)(2,1)} copy(bf16[128,4,16,128]{0,1,3,2:T(4,128)(2,1)} %bitcast.20) | data formatting | bytes 4194304 | tf_op jit(solution)/shard_map/all_to_all | solution.py:41
  136.2 0.7 slice.24
  136.9 81.6 %all_gather.3 = bf16[32,64,128]{2,1,0:T(8,128)(2,1)S(1)} all-gather(bf16[1,64,128]{2,1,0:T(8,128)(2,1)S(1)} %bitcast.22), channel_id=1, replica_groups=mesh['chan'=32,'freq'=16] {'chan'}, dimensions={0}, use_global_device_ids=true | all-gather | bytes 540672 | tf_op jit(solution)/shard_map/all_gather | solution.py:42
  218.6 1.0 fusion.40
  219.6 1.8 copy.16
  221.4 1.4 fusion.23
  222.7 1.4 fusion.19
  224.1 0.8 copy.17
  224.9 0.0 copy-start.2
  224.9 1.7 fusion.18
  226.6 0.0 copy-done.2
  226.6 0.4 fusion.17
  227.0 1.2 fusion.14
  (3 shorter events, 0.0 us)
Async XLA Ops:
  0.0 6.2 %copy-start.1 = (bf16[128,8192]{1,0:T(8,128)(2,1)S(1)}, bf16[128,8192]{1,0:T(8,128)(2,1)}, u32[]{:S(2)}) copy-start(bf16[128,8192]{1,0:T(8,128)(2,1)} %param.1) | copy-start | bytes 6291460
  91.5 35.1 %all-to-all-start = ((bf16[128,4,2048]{0,1,2:T(4,128)(2,1)}), bf16[128,4,2048]{0,1,2:T(4,128)(2,1)S(1)}, u32[]{:S(2)}, u32[]{:S(2)}) async-start(bf16[128,4,2048]{0,1,2:T(4,128)(2,1)} %copy.10), calls=%async_computation | async-start | bytes 4194304 | tf_op jit(solution)/shard_map/all_to_all | solution.py:41
  126.6 1.3 copy-start
  224.9 1.7 copy-start.2
where the time goes:
time: 232 us; the launch traced here: 228 us
  blocking collectives  81.6 us (35%)
  matrix products  75.2 us (32%)
  local copies, waits for them, and re-layouts  29.6 us (13%)
  waiting for transfers between devices  24.3 us (10%)
  starting transfers between devices  9.39 us (4%)
  other arithmetic  7.36 us (3%)
    all_gather x1, blocking collectives, local(): ref_spec = lax.all_gather(local_spec[:REF_DEV], 'chan', axis=0, tiled=True)  81.6 us
    dot_general x1, matrix products, local(): jnp.dot(windowed.reshape(rows * SEG_DEV, L), table, preferred_element_typ...  70.3 us
    all_to_all x1, waiting for transfers between devices, local(): lax.all_to_all(spectra, 'freq', split_axis=2, concat_axis=1, tiled=True)  24.3 us
    all_to_all x1, starting transfers between devices, local(): lax.all_to_all(spectra, 'freq', split_axis=2, concat_axis=1, tiled=True)  9.39 us
    reshape x2, local copies, waits for them, and re-layouts, local(): seg = signal.astype(jnp.float32).reshape(rows, SEG_DEV, L)  9.19 us
    all_to_all x2, local copies, waits for them, and re-layouts, local(): lax.all_to_all(spectra, 'freq', split_axis=2, concat_axis=1, tiled=True)  8.27 us
    reshape x2, local copies, waits for them, and re-layouts, local(): spectra = spectra.astype(jnp.bfloat16).reshape(rows, SEG_DEV, 2 * BINS)  6.4 us
  transfers between devices with their start and end apart: 1, of which 1 were waited for; matrix products, arithmetic and copies ran while one was open for 0% of the time, Pallas kernels for 0%

commit v1 on v0

v1 whole, which is shorter than its diff:
```python
import functools

import jax
import jax.numpy as jnp
import ml_dtypes
import numpy as np
from jax import lax
from jax.experimental import pallas as pl
from jax.experimental.pallas import tpu as pltpu
from jax.sharding import PartitionSpec as P

MESH = pl.DeviceIdType.MESH
L = 2048
BINS = 1024
SEG_DEV = 4
CH = 128
REFS = 32
SEGS = 64
Z_OFFSETS = (4, 8, 12, 1, 15, 2, 14)
NT = (((1,), (1,)), ((), ()))


def make_window():
    n = np.arange(L, dtype=np.float64)
    return (0.5 - 0.5 * np.cos(2.0 * np.pi * n / L)).astype(np.float32)


def make_table():
    core, chip, part, group, ri, b = np.ix_(*(np.arange(m) for m in (2, 8, 2, 8, 2, 4)))
    k = ((chip * 2 + core) * 64 + part * 32 + group * 4 + b + 0 * ri).reshape(2, 8, 2, 64)
    second = (ri + 0 * (core + chip + part + group + b)).reshape(2, 8, 2, 64)
    angle = 2.0 * np.pi * np.arange(L, dtype=np.float64) / L
    waves = np.stack([np.cos(angle), -np.sin(angle)]).astype(np.float32).astype(ml_dtypes.bfloat16)
    n = np.arange(L)
    return waves[second[..., None], (k[..., None] * n) % L]


def kernel(
    sig_hbm, tab_hbm, win_ref, out_ref,
    sig, sig2, tab, wnd, sbuf, data, rsend, rrecv, blocks, rf, lhs,
    sig_sem, tab_sem, xs_sem, xr_sem, bs_sem, br_sem, bl_sem,
    rs_sem, rr_sem, ys_sem, yr_sem, zs_sem, zr_sem, ready,
):
    c = lax.axis_index("chan")
    f = lax.axis_index("freq")
    z, yh = c // 2, c % 2
    core, q = f % 2, f // 2
    yl, x = q // 4, q % 4
    cls, za = z % 4, z // 4
    scale = np.float32(1.0 / (SEGS * np.sum(make_window().astype(np.float64) ** 2)))

    def chip(e, i):
        return (yl + i + 1 + e) % 2, (x + i + 2) % 4

    def source(e, i):
        return (yl + i + 1 + e) % 2, (x + 8 - i - 2) % 4

    def freq_of(yx):
        return (yx[0] * 4 + yx[1]) * 2 + core

    def zpeer(o):
        return ((z + o) % 16) * 2 + yh

    load_sig = pltpu.make_async_copy(sig_hbm, sig, sig_sem)
    load_sig.start()
    for d in range(8):
        ty, tx = chip(d // 4, d % 4)
        pltpu.make_async_copy(tab_hbm.at[core, ty * 4 + tx], tab.at[d], tab_sem.at[d]).start()

    barrier = pltpu.get_barrier_semaphore()
    for d in range(8):
        if d != 6:
            pl.semaphore_signal(
                barrier, inc=1, device_id=(c, freq_of(source(d // 4, d % 4))), device_id_type=MESH
            )
    partner = (c, f + 1 - 2 * core)
    ypartner = (z * 2 + 1 - yh, f)
    pl.semaphore_signal(barrier, inc=1, device_id=partner, device_id_type=MESH)
    pl.semaphore_signal(barrier, inc=1, device_id=ypartner, device_id_type=MESH)
    for o in Z_OFFSETS:
        @pl.when(z + o < 16)
        def _():
            pl.semaphore_signal(barrier, inc=1, device_id=(zpeer(o), f), device_id_type=MESH)

    def windowed(h, src, group):
        rows = pl.ds(pl.multiple_of(group * 16, 16), 16)
        for s in range(SEG_DEV):
            seg = src[rows, s * L:(s + 1) * L].astype(jnp.float32)
            mean = jnp.sum(seg, axis=1, keepdims=True) * np.float32(1.0 / L)
            wnd[h, s, rows, :] = ((seg - mean) * win_ref[...]).astype(jnp.bfloat16)

    def transform(h, e, p):
        t = tab[pl.ds(e * 4, 4), p].reshape(256, L)
        w = wnd[h].reshape(SEG_DEV * CH, L)
        spec = lax.dot_general(t, w, NT, preferred_element_type=jnp.float32)
        for i in range(4):
            for sp in range(2):
                pair = [
                    spec[i * 64:(i + 1) * 64, (2 * sp + k) * CH:(2 * sp + k + 1) * CH].reshape(8, 8, CH)
                    for k in range(2)
                ]
                sbuf[h, p, e * 4 + i, sp] = jnp.concatenate(pair, axis=1).astype(jnp.bfloat16)

    def bulk(h, p, e, i):
        return pltpu.make_async_remote_copy(
            src_ref=sbuf.at[h, p, e * 4 + i], dst_ref=data.at[p, q, h],
            send_sem=bs_sem.at[h, p, e * 4 + i], recv_sem=br_sem.at[h, p, e * 4 + i],
            device_id=(c, freq_of(chip(e, i))), device_id_type=MESH,
        )

    def bulk_in(h, p, e, i):
        sy, sx = source(e, i)
        return pltpu.make_async_remote_copy(
            src_ref=sbuf.at[h, p, e * 4 + i], dst_ref=data.at[p, sy * 4 + sx, h],
            send_sem=bs_sem.at[h, p, e * 4 + i], recv_sem=br_sem.at[h, p, e * 4 + i],
            device_id=(c, freq_of(chip(e, i))), device_id_type=MESH,
        )

    def own(h, p):
        return pltpu.make_async_copy(sbuf.at[h, p, 6], data.at[p, q, h], bl_sem.at[h, p])

    def send_bulk(h, p, e):
        for i in range(4):
            if e == 1 and i == 2:
                own(h, p).start()
            else:
                bulk(h, p, e, i).start()

    load_sig.wait()
    lax.fori_loop(0, 8, lambda g, _: (windowed(0, sig, g), 0)[1], 0)
    for d in range(8):
        pltpu.make_async_copy(tab_hbm.at[core, 0], tab.at[d], tab_sem.at[d]).wait()

    def own_chunk(ch, _):
        transform(0, ch % 2, ch // 2)
        return 0

    lax.fori_loop(0, 4, own_chunk, 0)

    early = [jnp.where(z + o >= 16, 1, 0) for o in Z_OFFSETS]
    pl.semaphore_wait(barrier, 9 + sum(early))
    for o in Z_OFFSETS:
        back = Z_OFFSETS.index(16 - o)

        @pl.when(z + o >= 16)
        def _():
            pl.semaphore_signal(ready.at[back], inc=1, device_id=(zpeer(o), f), device_id_type=MESH)

    def wait_ready(o):
        @pl.when(z + o < 16)
        def _():
            pl.semaphore_wait(ready.at[Z_OFFSETS.index(o)], 1)

    cross = [
        pltpu.make_async_remote_copy(
            src_ref=sig.at[rows], dst_ref=sig2.at[rows], send_sem=xs_sem.at[k], recv_sem=xr_sem.at[k],
            device_id=partner, device_id_type=MESH,
        )
        for k, rows in enumerate((pl.ds(0, 16), pl.ds(16, 112)))
    ]
    cross[0].start()
    cross[1].start()

    cross[0].wait_recv()
    windowed(1, sig2, 0)
    rows = [wnd[h, s, 0:16, :].astype(jnp.float32)[0:1] for h in range(2) for s in range(SEG_DEV)]
    wref = jnp.concatenate(rows + [jnp.zeros((8, L), jnp.float32)], axis=0).astype(jnp.bfloat16)
    refs_out = []
    for d in range(0, 8, 2):
        rspec = lax.dot_general(wref, tab[d:d + 2].reshape(256, L), NT, preferred_element_type=jnp.float32)
        rspec = rspec[0:8].astype(jnp.bfloat16).astype(jnp.float32)
        for k in range(2):
            if d + k == 6:
                rrecv[q] = rspec[:, k * 128:(k + 1) * 128]
            else:
                rsend[d + k] = rspec[:, k * 128:(k + 1) * 128]
                yx = chip((d + k) // 4, (d + k) % 4)
                copy = pltpu.make_async_remote_copy(
                    src_ref=rsend.at[d + k], dst_ref=rrecv.at[q],
                    send_sem=rs_sem.at[d + k], recv_sem=rr_sem.at[d + k],
                    device_id=(c, freq_of(yx)), device_id_type=MESH,
                )
                copy.start()
                refs_out.append((d + k, copy))

    for p in range(2):
        for e in range(2):
            send_bulk(0, p, e)

    for d, _ in refs_out:
        sy, sx = source(d // 4, d % 4)
        pltpu.make_async_remote_copy(
            src_ref=rsend.at[d], dst_ref=rrecv.at[sy * 4 + sx], send_sem=rs_sem.at[d], recv_sem=rr_sem.at[d],
            device_id=(c, freq_of(chip(d // 4, d % 4))), device_id_type=MESH,
        ).wait_recv()
    row = lax.broadcasted_iota(jnp.int32, (16, 128), 0)
    lane = lax.broadcasted_iota(jnp.int32, (16, 128), 1)
    diagonal = lane // 8 == row
    for g in range(4):
        a = rrecv[2 * g:2 * g + 2].reshape(16, 128)
        total = jnp.where(diagonal, a, 0.0)
        for d in range(1, 16):
            moved = jnp.where(diagonal, pltpu.roll(a, 8 * d, 1), 0.0)
            total = total + pltpu.roll(moved, 16 - d, 0)
        blocks[cls, za, yh, :, g * 128:(g + 1) * 128] = total.astype(jnp.bfloat16)

    ycopy = pltpu.make_async_remote_copy(
        src_ref=blocks.at[cls, za, yh], dst_ref=blocks.at[cls, za, yh], send_sem=ys_sem, recv_sem=yr_sem,
        device_id=ypartner, device_id_type=MESH,
    )
    ycopy.start()

    cross[1].wait_recv()
    lax.fori_loop(1, 8, lambda g, _: (windowed(1, sig2, g), 0)[1], 0)

    def zcopy(o, src, dst):
        k = Z_OFFSETS.index(o)
        return pltpu.make_async_remote_copy(
            src_ref=src, dst_ref=dst, send_sem=zs_sem.at[k], recv_sem=zr_sem.at[k],
            device_id=(zpeer(o), f), device_id_type=MESH,
        )

    pltpu.make_async_remote_copy(
        src_ref=blocks.at[cls, za, yh], dst_ref=blocks.at[cls, za, 1 - yh], send_sem=ys_sem, recv_sem=yr_sem,
        device_id=ypartner, device_id_type=MESH,
    ).wait_recv()
    sent = []
    for o in (4, 8, 12):
        wait_ready(o)
        copy = zcopy(o, blocks.at[cls, za], blocks.at[cls, za])
        copy.start()
        sent.append(copy)

    for p in range(2):
        for e in range(2):
            transform(1, e, p)
            send_bulk(1, p, e)

    for o in (4, 8, 12):
        zcopy(o, blocks.at[cls, za], blocks.at[cls, (za + 4 - o // 4) % 4]).wait_recv()
    for o in (1, 15, 2, 14):
        wait_ready(o)
        src = {1: blocks.at[cls], 15: blocks.at[cls], 2: blocks.at[cls, 0:2], 14: blocks.at[cls, 2:4]}[o]
        copy = zcopy(o, src, src)
        copy.start()
        sent.append(copy)
    other = (cls + 2) % 4
    for o, got in (
        (1, blocks.at[(cls + 3) % 4]), (15, blocks.at[(cls + 1) % 4]),
        (2, blocks.at[other, 0:2]), (14, blocks.at[other, 2:4]),
    ):
        zcopy(o, got, got).wait_recv()

    for r in range(REFS):
        zr, yr = r // 2, r % 2
        block = blocks[zr % 4, zr // 4, yr].astype(jnp.float32)
        for g in range(4):
            rf[g, r * 16:(r + 1) * 16, :] = block[:, g * 128:(g + 1) * 128]

    wide = lax.broadcasted_iota(jnp.int32, (REFS, 512), 1)

    def build(kg, _):
        re = jnp.concatenate([rf[g, pl.ds(kg, REFS, stride=16), :] for g in range(4)], axis=1)
        im = jnp.where(wide % 8 < 4, -pltpu.roll(re, 508, 1), pltpu.roll(re, 4, 1))
        for b in range(4):
            keep = wide % 4 == b
            lhs[kg, b * 64:b * 64 + 32, :] = jnp.where(keep, re, 0.0).astype(jnp.bfloat16)
            lhs[kg, b * 64 + 32:b * 64 + 64, :] = jnp.where(keep, im, 0.0).astype(jnp.bfloat16)
        return 0

    lax.fori_loop(0, 16, build, 0)

    for p in range(2):
        for h in range(2):
            own(h, p).wait()
            for e in range(2):
                for i in range(4):
                    if not (e == 1 and i == 2):
                        bulk_in(h, p, e, i).wait_recv()

        def products(kg, _):
            right = data[p, :, :, :, kg].reshape(512, CH)
            both = jnp.dot(lhs[p * 8 + kg], right, preferred_element_type=jnp.float32) * scale
            both = both.astype(jnp.bfloat16)
            for b in range(4):
                for ri in range(2):
                    out_ref[ri, (p * 8 + kg) * 4 + b] = both[(b * 2 + ri) * 32:(b * 2 + ri + 1) * 32]
            return 0

        lax.fori_loop(0, 8, products, 0)

    cross[0].wait_send()
    cross[1].wait_send()
    ycopy.wait_send()
    for _, copy in refs_out:
        copy.wait_send()
    for copy in sent:
        copy.wait_send()
    for h in range(2):
        for p in range(2):
            for e in range(2):
                for i in range(4):
                    if not (e == 1 and i == 2):
                        bulk(h, p, e, i).wait_send()


def local(signal, table, window):
    bf16, f32 = jnp.bfloat16, jnp.float32
    dma = pltpu.SemaphoreType.DMA
    return pl.pallas_call(
        kernel,
        out_shape=jax.ShapeDtypeStruct((2, 64, REFS, CH), bf16),
        in_specs=[
            pl.BlockSpec(memory_space=pl.ANY),
            pl.BlockSpec(memory_space=pl.ANY),
            pl.BlockSpec(memory_space=pltpu.VMEM),
        ],
        out_specs=pl.BlockSpec(memory_space=pltpu.VMEM),
        scratch_shapes=[
            pltpu.VMEM((CH, SEG_DEV * L), bf16),
            pltpu.VMEM((CH, SEG_DEV * L), bf16),
            pltpu.VMEM((8, 2, 64, L), bf16),
            pltpu.VMEM((2, SEG_DEV, CH, L), bf16),
            pltpu.VMEM((2, 2, 8, 2, 8, 16, CH), bf16),
            pltpu.VMEM((2, 8, 2, 2, 8, 16, CH), bf16),
            pltpu.VMEM((8, 8, 128), f32),
            pltpu.VMEM((8, 8, 128), f32),
            pltpu.VMEM((4, 4, 2, 16, 512), bf16),
            pltpu.VMEM((4, REFS * 16, 128), f32),
            pltpu.VMEM((16, 256, 512), bf16),
            dma, dma((8,)), dma((2,)), dma((2,)), dma((2, 2, 8)), dma((2, 2, 8)), dma((2, 2)),
            dma((8,)), dma((8,)), dma, dma, dma((7,)), dma((7,)), pltpu.SemaphoreType.REGULAR((7,)),
        ],
        compiler_params=pltpu.CompilerParams(
            collective_id=0, has_side_effects=True, vmem_limit_bytes=52 * 2**20
        ),
        cost_estimate=pl.CostEstimate(flops=5 * 10**9, bytes_accessed=8 * 10**6, transcendentals=0),
        name="cross_spectra",
    )(signal, table, window)


def solution(mesh):
    table = make_table()
    window = make_window()[None, :]

    def whole(signal):
        return local(signal, jnp.asarray(table), jnp.asarray(window))

    return jax.shard_map(
        whole, mesh=mesh, in_specs=(P("chan", "freq"),), out_specs=P(None, "freq", None, "chan"), check_vma=False
    )
```

time: 232 us -> 61.2 us (0.26); the launches traced: 228 us -> 61 us
  blocking collectives: 81.6 us -> 0 us
  matrix products: 75.2 us -> 0 us
  Pallas kernels: 0 us -> 59.4 us
  local copies, waits for them, and re-layouts: 29.6 us -> 1.67 us
  waiting for transfers between devices: 24.3 us -> 0 us
  starting transfers between devices: 9.39 us -> 0 us
  other arithmetic: 7.36 us -> 0 us
    all_gather x1 -> x0, blocking collectives: 81.6 us -> none  [local(): ref_spec = lax.all_gather(local_spec[:REF_DEV], 'chan', axis=0, tiled=True)]
    dot_general x5 -> x0, matrix products: 75.2 us -> none  [the longest x1 70.3 us: local(): jnp.dot(windowed.reshape(rows * SEG_DEV, L), table, preferred_element_typ...]
    pallas_call x0 -> x1, Pallas kernels: none -> 59.4 us  [local(): pl.pallas_call(kernel, out_shape=jax.ShapeDtypeStruct((2, 64, REFS, CH),...]
    all_to_all x1 -> x0, waiting for transfers between devices: 24.3 us -> none  [local(): lax.all_to_all(spectra, 'freq', split_axis=2, concat_axis=1, tiled=True)]
    reshape x4 -> x0, local copies, waits for them, and re-layouts: 15.6 us -> none  [the longest x2 9.19 us: local(): seg = signal.astype(jnp.float32).reshape(rows, SEG_DEV, L)]
    all_to_all x1 -> x0, starting transfers between devices: 9.39 us -> none  [local(): lax.all_to_all(spectra, 'freq', split_axis=2, concat_axis=1, tiled=True)]
    all_to_all x2 -> x0, local copies, waits for them, and re-layouts: 8.27 us -> none  [local(): lax.all_to_all(spectra, 'freq', split_axis=2, concat_axis=1, tiled=True)]
    reduce_sum x2 -> x0, other arithmetic: 3.47 us -> none  [the longest x1 2.82 us: local(): seg = seg - jnp.mean(seg, axis=2, keepdims=True)]
  transfers between devices with their start and end apart: 1 -> 0, of which waited for: 1 -> 0; matrix products, arithmetic and copies ran while one was open for 0% -> 0% of each run, Pallas kernels for 0% -> 0%
where the time goes in v1:
time: 61.2 us; the launch traced here: 61 us
  Pallas kernels  59.4 us (97%)
  local copies, waits for them, and re-layouts  1.67 us (3%)
    pallas_call x1, Pallas kernels, local(): pl.pallas_call(kernel, out_shape=jax.ShapeDtypeStruct((2, 64, REFS, CH),...  59.4 us
    unnamed x3, local copies, waits for them, and re-layouts  1.67 us

profile of v1, /device:TPU:6, one launch (start us, length us, event | category | flops | bytes accessed | tf_op | source)
XLA Modules:
  0.0 61.0 jit_solution(10069632601690692140)
XLA Ops:
  0.0 0.0 copy-start
  0.0 0.7 %copy-done = f32[1,2048]{1,0:T(1,128)S(1)} copy-done((f32[1,2048]{1,0:T(1,128)S(1)}, f32[1,2048]{1,0:T(1,128)}, u32[]{:S(2)}) %copy-start) | copy-done | bytes 8216
  0.7 59.4 %cross_spectra.1 = bf16[2,64,32,128]{3,2,1,0:T(8,128)(2,1)S(1)} custom-call(bf16[128,8192]{1,0:T(8,128)(2,1)} %sig_hbm.1, bf16[2,8,2,64,2048]{4,3,2,1,0:T(8,128)(2,1)} %constant.4.clone.tab_hbm, f32[1,2048]{1,0:T(1,128)S(1)} %copy-done), custom_call_target="tpu_custom_call" | custom-call | flops 5000000000 | bytes 8000000 | tf_op jit(solution)/shard_map/cross_spectra/pallas_call | solution.py:310
  60.1 1.0 %copy.5 = bf16[2,64,32,128]{3,2,1,0:T(8,128)(2,1)} copy(bf16[2,64,32,128]{3,2,1,0:T(8,128)(2,1)S(1)} %cross_spectra.1) | data formatting | bytes 2097152
Async XLA Ops:
  0.0 0.7 %copy-start = (f32[1,2048]{1,0:T(1,128)S(1)}, f32[1,2048]{1,0:T(1,128)}, u32[]{:S(2)}) copy-start(f32[1,2048]{1,0:T(1,128)} %constant.5.clone.win_ref) | copy-start | bytes 24580

commit v2 on v1

--- a/solution.py
+++ b/solution.py
@@ -36,10 +36,10 @@
 
 
 def kernel(
-    sig_hbm, tab_hbm, win_ref, out_ref,
-    sig, sig2, tab, wnd, sbuf, data, rsend, rrecv, blocks, rf, lhs,
-    sig_sem, tab_sem, xs_sem, xr_sem, bs_sem, br_sem, bl_sem,
-    rs_sem, rr_sem, ys_sem, yr_sem, zs_sem, zr_sem, ready,
+    sig_hbm, tab_hbm, win_hbm, out_hbm,
+    win_ref, out_ref, sig, sig2, tab, wnd, sbuf, data, rsend, rrecv, blocks, rf, lhs,
+    win_sem, sig_sem, tab_sem, xs_sem, xr_sem, bs_sem, br_sem, bl_sem,
+    rs_sem, rr_sem, zs_sem, zr_sem, out_sem, ready,
 ):
     c = lax.axis_index("chan")
     f = lax.axis_index("freq")
@@ -63,20 +63,21 @@
 
     load_sig = pltpu.make_async_copy(sig_hbm, sig, sig_sem)
     load_sig.start()
+    load_win = pltpu.make_async_copy(win_hbm, win_ref, win_sem)
+    load_win.start()
     for d in range(8):
         ty, tx = chip(d // 4, d % 4)
         pltpu.make_async_copy(tab_hbm.at[core, ty * 4 + tx], tab.at[d], tab_sem.at[d]).start()
 
     barrier = pltpu.get_barrier_semaphore()
+    partner = (c, f + 1 - 2 * core)
+    other_c = z * 2 + 1 - yh
     for d in range(8):
+        sender = freq_of(source(d // 4, d % 4))
         if d != 6:
-            pl.semaphore_signal(
-                barrier, inc=1, device_id=(c, freq_of(source(d // 4, d % 4))), device_id_type=MESH
-            )
-    partner = (c, f + 1 - 2 * core)
-    ypartner = (z * 2 + 1 - yh, f)
+            pl.semaphore_signal(barrier, inc=1, device_id=(c, sender), device_id_type=MESH)
+        pl.semaphore_signal(barrier, inc=1, device_id=(other_c, sender), device_id_type=MESH)
     pl.semaphore_signal(barrier, inc=1, device_id=partner, device_id_type=MESH)
-    pl.semaphore_signal(barrier, inc=1, device_id=ypartner, device_id_type=MESH)
     for o in Z_OFFSETS:
         @pl.when(z + o < 16)
         def _():
@@ -126,19 +127,12 @@
             else:
                 bulk(h, p, e, i).start()
 
+    load_win.wait()
     load_sig.wait()
     lax.fori_loop(0, 8, lambda g, _: (windowed(0, sig, g), 0)[1], 0)
-    for d in range(8):
-        pltpu.make_async_copy(tab_hbm.at[core, 0], tab.at[d], tab_sem.at[d]).wait()
-
-    def own_chunk(ch, _):
-        transform(0, ch % 2, ch // 2)
-        return 0
-
-    lax.fori_loop(0, 4, own_chunk, 0)
 
     early = [jnp.where(z + o >= 16, 1, 0) for o in Z_OFFSETS]
-    pl.semaphore_wait(barrier, 9 + sum(early))
+    pl.semaphore_wait(barrier, 16 + sum(early))
     for o in Z_OFFSETS:
         back = Z_OFFSETS.index(16 - o)
 
@@ -161,57 +155,53 @@
     cross[0].start()
     cross[1].start()
 
+    for d in range(8):
+        pltpu.make_async_copy(tab_hbm.at[core, 0], tab.at[d], tab_sem.at[d]).wait()
+    lax.fori_loop(0, 2, lambda e, _: (transform(0, e, 0), 0)[1], 0)
+
     cross[0].wait_recv()
     windowed(1, sig2, 0)
     rows = [wnd[h, s, 0:16, :].astype(jnp.float32)[0:1] for h in range(2) for s in range(SEG_DEV)]
     wref = jnp.concatenate(rows + [jnp.zeros((8, L), jnp.float32)], axis=0).astype(jnp.bfloat16)
-    refs_out = []
+
+    def ref_copy(w, d, slot):
+        return pltpu.make_async_remote_copy(
+            src_ref=rsend.at[d], dst_ref=rrecv.at[w, slot], send_sem=rs_sem.at[w, d], recv_sem=rr_sem.at[w, d],
+            device_id=((c, other_c)[w], freq_of(chip(d // 4, d % 4))), device_id_type=MESH,
+        )
+
+    pairs = [(w, d) for d in range(8) for w in range(2) if (w, d) != (0, 6)]
     for d in range(0, 8, 2):
         rspec = lax.dot_general(wref, tab[d:d + 2].reshape(256, L), NT, preferred_element_type=jnp.float32)
         rspec = rspec[0:8].astype(jnp.bfloat16).astype(jnp.float32)
         for k in range(2):
+            rsend[d + k] = rspec[:, k * 128:(k + 1) * 128]
             if d + k == 6:
-                rrecv[q] = rspec[:, k * 128:(k + 1) * 128]
-            else:
-                rsend[d + k] = rspec[:, k * 128:(k + 1) * 128]
-                yx = chip((d + k) // 4, (d + k) % 4)
-                copy = pltpu.make_async_remote_copy(
-                    src_ref=rsend.at[d + k], dst_ref=rrecv.at[q],
-                    send_sem=rs_sem.at[d + k], recv_sem=rr_sem.at[d + k],
-                    device_id=(c, freq_of(yx)), device_id_type=MESH,
-                )
-                copy.start()
-                refs_out.append((d + k, copy))
-
-    for p in range(2):
-        for e in range(2):
-            send_bulk(0, p, e)
-
-    for d, _ in refs_out:
+                rrecv[0, q] = rspec[:, k * 128:(k + 1) * 128]
+            for w in range(2):
+                if (w, d + k) != (0, 6):
+                    ref_copy(w, d + k, q).start()
+
+    for e in range(2):
+        send_bulk(0, 0, e)
+    for e in range(2):
+        transform(0, e, 1)
+        send_bulk(0, 1, e)
+
+    for w, d in pairs:
         sy, sx = source(d // 4, d % 4)
-        pltpu.make_async_remote_copy(
-            src_ref=rsend.at[d], dst_ref=rrecv.at[sy * 4 + sx], send_sem=rs_sem.at[d], recv_sem=rr_sem.at[d],
-            device_id=(c, freq_of(chip(d // 4, d % 4))), device_id_type=MESH,
-        ).wait_recv()
+        ref_copy(w, d, sy * 4 + sx).wait_recv()
     row = lax.broadcasted_iota(jnp.int32, (16, 128), 0)
     lane = lax.broadcasted_iota(jnp.int32, (16, 128), 1)
     diagonal = lane // 8 == row
-    for g in range(4):
-        a = rrecv[2 * g:2 * g + 2].reshape(16, 128)
-        total = jnp.where(diagonal, a, 0.0)
-        for d in range(1, 16):
-            moved = jnp.where(diagonal, pltpu.roll(a, 8 * d, 1), 0.0)
-            total = total + pltpu.roll(moved, 16 - d, 0)
-        blocks[cls, za, yh, :, g * 128:(g + 1) * 128] = total.astype(jnp.bfloat16)
-
-    ycopy = pltpu.make_async_remote_copy(
-        src_ref=blocks.at[cls, za, yh], dst_ref=blocks.at[cls, za, yh], send_sem=ys_sem, recv_sem=yr_sem,
-        device_id=ypartner, device_id_type=MESH,
-    )
-    ycopy.start()
-
-    cross[1].wait_recv()
-    lax.fori_loop(1, 8, lambda g, _: (windowed(1, sig2, g), 0)[1], 0)
+    for w, y_of in ((0, yh), (1, 1 - yh)):
+        for g in range(4):
+            a = rrecv[w, 2 * g:2 * g + 2].reshape(16, 128)
+            total = jnp.where(diagonal, a, 0.0)
+            for d in range(1, 16):
+                moved = jnp.where(diagonal, pltpu.roll(a, 8 * d, 1), 0.0)
+                total = total + pltpu.roll(moved, 16 - d, 0)
+            blocks[cls, za, y_of, :, g * 128:(g + 1) * 128] = total.astype(jnp.bfloat16)
 
     def zcopy(o, src, dst):
         k = Z_OFFSETS.index(o)
@@ -220,23 +210,21 @@
             device_id=(zpeer(o), f), device_id_type=MESH,
         )
 
-    pltpu.make_async_remote_copy(
-        src_ref=blocks.at[cls, za, yh], dst_ref=blocks.at[cls, za, 1 - yh], send_sem=ys_sem, recv_sem=yr_sem,
-        device_id=ypartner, device_id_type=MESH,
-    ).wait_recv()
     sent = []
-    for o in (4, 8, 12):
+    for o in (4, 12, 8):
         wait_ready(o)
         copy = zcopy(o, blocks.at[cls, za], blocks.at[cls, za])
         copy.start()
         sent.append(copy)
 
+    cross[1].wait_recv()
+    lax.fori_loop(1, 8, lambda g, _: (windowed(1, sig2, g), 0)[1], 0)
     for p in range(2):
         for e in range(2):
             transform(1, e, p)
             send_bulk(1, p, e)
 
-    for o in (4, 8, 12):
+    for o in (4, 12, 8):
         zcopy(o, blocks.at[cls, za], blocks.at[cls, (za + 4 - o // 4) % 4]).wait_recv()
     for o in (1, 15, 2, 14):
         wait_ready(o)
@@ -268,9 +256,12 @@
             lhs[kg, b * 64 + 32:b * 64 + 64, :] = jnp.where(keep, im, 0.0).astype(jnp.bfloat16)
         return 0
 
-    lax.fori_loop(0, 16, build, 0)
+    def store_out(p):
+        half = pl.ds(p * 32, 32)
+        return pltpu.make_async_copy(out_ref.at[:, half], out_hbm.at[:, half], out_sem.at[p])
 
     for p in range(2):
+        lax.fori_loop(p * 8, p * 8 + 8, build, 0)
         for h in range(2):
             own(h, p).wait()
             for e in range(2):
@@ -278,22 +269,24 @@
                     if not (e == 1 and i == 2):
                         bulk_in(h, p, e, i).wait_recv()
 
-        def products(kg, _):
-            right = data[p, :, :, :, kg].reshape(512, CH)
-            both = jnp.dot(lhs[p * 8 + kg], right, preferred_element_type=jnp.float32) * scale
-            both = both.astype(jnp.bfloat16)
-            for b in range(4):
-                for ri in range(2):
-                    out_ref[ri, (p * 8 + kg) * 4 + b] = both[(b * 2 + ri) * 32:(b * 2 + ri + 1) * 32]
+        def products(step, _):
+            for j in range(4):
+                kg = step * 4 + j
+                right = data[p, :, :, :, kg].reshape(512, CH)
+                both = jnp.dot(lhs[p * 8 + kg], right, preferred_element_type=jnp.float32) * scale
+                both = both.astype(jnp.bfloat16)
+                for b in range(4):
+                    for ri in range(2):
+                        out_ref[ri, (p * 8 + kg) * 4 + b] = both[(b * 2 + ri) * 32:(b * 2 + ri + 1) * 32]
             return 0
 
-        lax.fori_loop(0, 8, products, 0)
+        lax.fori_loop(0, 2, products, 0)
+        store_out(p).start()
 
     cross[0].wait_send()
     cross[1].wait_send()
-    ycopy.wait_send()
-    for _, copy in refs_out:
-        copy.wait_send()
+    for w, d in pairs:
+        ref_copy(w, d, q).wait_send()
     for copy in sent:
         copy.wait_send()
     for h in range(2):
@@ -302,6 +295,8 @@
                 for i in range(4):
                     if not (e == 1 and i == 2):
                         bulk(h, p, e, i).wait_send()
+    store_out(0).wait()
+    store_out(1).wait()
 
 
 def local(signal, table, window):
@@ -313,10 +308,12 @@
         in_specs=[
             pl.BlockSpec(memory_space=pl.ANY),
             pl.BlockSpec(memory_space=pl.ANY),
-            pl.BlockSpec(memory_space=pltpu.VMEM),
+            pl.BlockSpec(memory_space=pl.ANY),
         ],
-        out_specs=pl.BlockSpec(memory_space=pltpu.VMEM),
+        out_specs=pl.BlockSpec(memory_space=pl.ANY),
         scratch_shapes=[
+            pltpu.VMEM((1, L), f32),
+            pltpu.VMEM((2, 64, REFS, CH), bf16),
             pltpu.VMEM((CH, SEG_DEV * L), bf16),
             pltpu.VMEM((CH, SEG_DEV * L), bf16),
             pltpu.VMEM((8, 2, 64, L), bf16),
@@ -324,12 +321,12 @@
             pltpu.VMEM((2, 2, 8, 2, 8, 16, CH), bf16),
             pltpu.VMEM((2, 8, 2, 2, 8, 16, CH), bf16),
             pltpu.VMEM((8, 8, 128), f32),
-            pltpu.VMEM((8, 8, 128), f32),
+            pltpu.VMEM((2, 8, 8, 128), f32),
             pltpu.VMEM((4, 4, 2, 16, 512), bf16),
             pltpu.VMEM((4, REFS * 16, 128), f32),
             pltpu.VMEM((16, 256, 512), bf16),
-            dma, dma((8,)), dma((2,)), dma((2,)), dma((2, 2, 8)), dma((2, 2, 8)), dma((2, 2)),
-            dma((8,)), dma((8,)), dma, dma, dma((7,)), dma((7,)), pltpu.SemaphoreType.REGULAR((7,)),
+            dma, dma, dma((8,)), dma((2,)), dma((2,)), dma((2, 2, 8)), dma((2, 2, 8)), dma((2, 2)),
+            dma((2, 8)), dma((2, 8)), dma((7,)), dma((7,)), dma((2,)), pltpu.SemaphoreType.REGULAR((7,)),
         ],
         compiler_params=pltpu.CompilerParams(
             collective_id=0, has_side_effects=True, vmem_limit_bytes=52 * 2**20

time: 61.2 us -> 45.7 us (0.75)
  the two profiles are of different devices: /device:TPU:6 before, /device:TPU:2 now
where the time goes in v2:
time: 45.7 us; the launch traced here: 45.6 us
  Pallas kernels  43.9 us (96%)
  local copies, waits for them, and re-layouts  1.67 us (4%)
    pallas_call x1, Pallas kernels, local(): pl.pallas_call(kernel, out_shape=jax.ShapeDtypeStruct((2, 64, REFS, CH),...  43.9 us
    unnamed x3, local copies, waits for them, and re-layouts  1.67 us

profile of v2, /device:TPU:2, one launch (start us, length us, event | category | flops | bytes accessed | tf_op | source)
XLA Modules:
  0.0 45.6 jit_solution(11820669226256276281)
XLA Ops:
  0.0 0.0 copy-start
  0.0 0.7 %copy-done = f32[1,2048]{1,0:T(1,128)S(1)} copy-done((f32[1,2048]{1,0:T(1,128)S(1)}, f32[1,2048]{1,0:T(1,128)}, u32[]{:S(2)}) %copy-start) | copy-done | bytes 8216
  0.7 43.9 %cross_spectra.1 = bf16[2,64,32,128]{3,2,1,0:T(8,128)(2,1)S(1)} custom-call(bf16[128,8192]{1,0:T(8,128)(2,1)} %sig_hbm.1, bf16[2,8,2,64,2048]{4,3,2,1,0:T(8,128)(2,1)} %constant.4.clone.tab_hbm, f32[1,2048]{1,0:T(1,128)S(1)} %copy-done), custom_call_target="tpu_custom_call" | custom-call | flops 5000000000 | bytes 8000000 | tf_op jit(solution)/shard_map/cross_spectra/pallas_call | solution.py:305
  44.6 1.0 %copy.5 = bf16[2,64,32,128]{3,2,1,0:T(8,128)(2,1)} copy(bf16[2,64,32,128]{3,2,1,0:T(8,128)(2,1)S(1)} %cross_spectra.1) | data formatting | bytes 2097152
Async XLA Ops:
  0.0 0.7 %copy-start = (f32[1,2048]{1,0:T(1,128)S(1)}, f32[1,2048]{1,0:T(1,128)}, u32[]{:S(2)}) copy-start(f32[1,2048]{1,0:T(1,128)} %constant.5.clone.win_hbm) | copy-start | bytes 24580

commit v3 on v2

--- a/solution.py
+++ b/solution.py
@@ -38,8 +38,9 @@
 def kernel(
     sig_hbm, tab_hbm, win_hbm, out_hbm,
     win_ref, out_ref, sig, sig2, tab, wnd, sbuf, data, rsend, rrecv, blocks, rf, lhs,
-    win_sem, sig_sem, tab_sem, xs_sem, xr_sem, bs_sem, br_sem, bl_sem,
-    rs_sem, rr_sem, zs_sem, zr_sem, out_sem, ready,
+    win_sem, sig_sem, tab_sem, cs_sem, cr_sem, bl_sem,
+    ys_sem, yr_sem, xs_sem, xr_sem, rs_sem, rr_sem,
+    zs_sem, zr_sem, zzs_sem, zzr_sem, out_sem, ready,
 ):
     c = lax.axis_index("chan")
     f = lax.axis_index("freq")
@@ -50,10 +51,10 @@
     scale = np.float32(1.0 / (SEGS * np.sum(make_window().astype(np.float64) ** 2)))
 
     def chip(e, i):
-        return (yl + i + 1 + e) % 2, (x + i + 2) % 4
+        return (yl + 1 - e) % 2, (x + i) % 4
 
     def source(e, i):
-        return (yl + i + 1 + e) % 2, (x + 8 - i - 2) % 4
+        return (yl + 1 - e) % 2, (x + 4 - i) % 4
 
     def freq_of(yx):
         return (yx[0] * 4 + yx[1]) * 2 + core
@@ -74,7 +75,7 @@
     other_c = z * 2 + 1 - yh
     for d in range(8):
         sender = freq_of(source(d // 4, d % 4))
-        if d != 6:
+        if d != 4:
             pl.semaphore_signal(barrier, inc=1, device_id=(c, sender), device_id_type=MESH)
         pl.semaphore_signal(barrier, inc=1, device_id=(other_c, sender), device_id_type=MESH)
     pl.semaphore_signal(barrier, inc=1, device_id=partner, device_id_type=MESH)
@@ -102,34 +103,55 @@
                 ]
                 sbuf[h, p, e * 4 + i, sp] = jnp.concatenate(pair, axis=1).astype(jnp.bfloat16)
 
-    def bulk(h, p, e, i):
+    other_q = (1 - yl) * 4
+
+    def along(i):
+        return (c, freq_of((yl, (x + i) % 4)))
+
+    def own(h, p):
+        return pltpu.make_async_copy(sbuf.at[h, p, 4], data.at[p, q, h], bl_sem.at[h, p])
+
+    def over_y(h, p, i, slot):
         return pltpu.make_async_remote_copy(
-            src_ref=sbuf.at[h, p, e * 4 + i], dst_ref=data.at[p, q, h],
-            send_sem=bs_sem.at[h, p, e * 4 + i], recv_sem=br_sem.at[h, p, e * 4 + i],
-            device_id=(c, freq_of(chip(e, i))), device_id_type=MESH,
-        )
-
-    def bulk_in(h, p, e, i):
-        sy, sx = source(e, i)
+            src_ref=sbuf.at[h, p, i], dst_ref=data.at[p, slot, h],
+            send_sem=ys_sem.at[h, p, i], recv_sem=yr_sem.at[h, p, i],
+            device_id=(c, freq_of((1 - yl, (x + i) % 4))), device_id_type=MESH,
+        )
+
+    def over_x(h, p, i, slot):
         return pltpu.make_async_remote_copy(
-            src_ref=sbuf.at[h, p, e * 4 + i], dst_ref=data.at[p, sy * 4 + sx, h],
-            send_sem=bs_sem.at[h, p, e * 4 + i], recv_sem=br_sem.at[h, p, e * 4 + i],
-            device_id=(c, freq_of(chip(e, i))), device_id_type=MESH,
-        )
-
-    def own(h, p):
-        return pltpu.make_async_copy(sbuf.at[h, p, 6], data.at[p, q, h], bl_sem.at[h, p])
-
-    def send_bulk(h, p, e):
+            src_ref=sbuf.at[h, p, 4 + i], dst_ref=data.at[p, slot, h],
+            send_sem=xs_sem.at[h, p, i], recv_sem=xr_sem.at[h, p, i],
+            device_id=along(i), device_id_type=MESH,
+        )
+
+    def send(h, p):
+        own(h, p).start()
+        for i in (2, 1, 3):
+            over_y(h, p, i, q).start()
+            over_x(h, p, i, q).start()
+        over_y(h, p, 0, q).start()
+
+    def receive(h, p):
+        own(h, p).wait()
+        for i in (1, 2, 3):
+            over_x(h, p, i, yl * 4 + (x + 4 - i) % 4).wait_recv()
         for i in range(4):
-            if e == 1 and i == 2:
-                own(h, p).start()
-            else:
-                bulk(h, p, e, i).start()
+            over_y(h, p, i, other_q + (x + 4 - i) % 4).wait_recv()
 
     load_win.wait()
     load_sig.wait()
     lax.fori_loop(0, 8, lambda g, _: (windowed(0, sig, g), 0)[1], 0)
+
+    for d in range(8):
+        pltpu.make_async_copy(tab_hbm.at[core, 0], tab.at[d], tab_sem.at[d]).wait()
+
+    def chunk(n, _):
+        transform(0, n % 2, n // 2)
+        return 0
+
+    ahead = jnp.where((z == 0) & (c + f > 0), 4, 0)
+    lax.fori_loop(0, ahead, chunk, 0)
 
     early = [jnp.where(z + o >= 16, 1, 0) for o in Z_OFFSETS]
     pl.semaphore_wait(barrier, 16 + sum(early))
@@ -147,7 +169,7 @@
 
     cross = [
         pltpu.make_async_remote_copy(
-            src_ref=sig.at[rows], dst_ref=sig2.at[rows], send_sem=xs_sem.at[k], recv_sem=xr_sem.at[k],
+            src_ref=sig.at[rows], dst_ref=sig2.at[rows], send_sem=cs_sem.at[k], recv_sem=cr_sem.at[k],
             device_id=partner, device_id_type=MESH,
         )
         for k, rows in enumerate((pl.ds(0, 16), pl.ds(16, 112)))
@@ -155,9 +177,8 @@
     cross[0].start()
     cross[1].start()
 
-    for d in range(8):
-        pltpu.make_async_copy(tab_hbm.at[core, 0], tab.at[d], tab_sem.at[d]).wait()
-    lax.fori_loop(0, 2, lambda e, _: (transform(0, e, 0), 0)[1], 0)
+    late = z >= 8
+    lax.fori_loop(jnp.minimum(ahead, 2), 2, chunk, 0)
 
     cross[0].wait_recv()
     windowed(1, sig2, 0)
@@ -170,23 +191,21 @@
             device_id=((c, other_c)[w], freq_of(chip(d // 4, d % 4))), device_id_type=MESH,
         )
 
-    pairs = [(w, d) for d in range(8) for w in range(2) if (w, d) != (0, 6)]
+    pairs = [(w, d) for d in range(8) for w in range(2) if (w, d) != (0, 4)]
     for d in range(0, 8, 2):
         rspec = lax.dot_general(wref, tab[d:d + 2].reshape(256, L), NT, preferred_element_type=jnp.float32)
         rspec = rspec[0:8].astype(jnp.bfloat16).astype(jnp.float32)
         for k in range(2):
             rsend[d + k] = rspec[:, k * 128:(k + 1) * 128]
-            if d + k == 6:
+            if d + k == 4:
                 rrecv[0, q] = rspec[:, k * 128:(k + 1) * 128]
             for w in range(2):
-                if (w, d + k) != (0, 6):
+                if (w, d + k) != (0, 4):
                     ref_copy(w, d + k, q).start()
 
-    for e in range(2):
-        send_bulk(0, 0, e)
-    for e in range(2):
-        transform(0, e, 1)
-        send_bulk(0, 1, e)
+    send(0, 0)
+    lax.fori_loop(jnp.maximum(ahead, 2), 4, chunk, 0)
+    send(0, 1)
 
     for w, d in pairs:
         sy, sx = source(d // 4, d % 4)
@@ -203,41 +222,76 @@
                 total = total + pltpu.roll(moved, 16 - d, 0)
             blocks[cls, za, y_of, :, g * 128:(g + 1) * 128] = total.astype(jnp.bfloat16)
 
-    def zcopy(o, src, dst):
-        k = Z_OFFSETS.index(o)
+    def far(j, slot):
         return pltpu.make_async_remote_copy(
-            src_ref=src, dst_ref=dst, send_sem=zs_sem.at[k], recv_sem=zr_sem.at[k],
+            src_ref=blocks.at[cls, za], dst_ref=blocks.at[cls, slot], send_sem=zs_sem.at[j], recv_sem=zr_sem.at[j],
+            device_id=(zpeer(4 * j), f), device_id_type=MESH,
+        )
+
+    def near(o, a, of):
+        k = (1, 15, 2, 14).index(o)
+        return pltpu.make_async_remote_copy(
+            src_ref=blocks.at[of, a], dst_ref=blocks.at[of, a],
+            send_sem=zzs_sem.at[k, a], recv_sem=zzr_sem.at[k, a],
             device_id=(zpeer(o), f), device_id_type=MESH,
         )
 
-    sent = []
-    for o in (4, 12, 8):
-        wait_ready(o)
-        copy = zcopy(o, blocks.at[cls, za], blocks.at[cls, za])
-        copy.start()
-        sent.append(copy)
+    def spread():
+        for o in (4, 12, 8):
+            wait_ready(o)
+            far(o // 4, za).start()
+
+    @pl.when(z >= 4)
+    def _():
+        spread()
+
+    def forward():
+        for o in (1, 15, 2, 14):
+            wait_ready(o)
+        for o in (1, 15):
+            near(o, za, cls).start()
+
+        @pl.when(za < 2)
+        def _():
+            near(2, za, cls).start()
+
+        @pl.when(za >= 2)
+        def _():
+            near(14, za, cls).start()
+
+        for a in (0, 1, 3, 2):
+            @pl.when(za != a)
+            def _():
+                far((za + 4 - a) % 4, a).wait_recv()
+                for o in (1, 15, 2 if a < 2 else 14):
+                    near(o, a, cls).start()
 
     cross[1].wait_recv()
     lax.fori_loop(1, 8, lambda g, _: (windowed(1, sig2, g), 0)[1], 0)
-    for p in range(2):
-        for e in range(2):
-            transform(1, e, p)
-            send_bulk(1, p, e)
-
-    for o in (4, 12, 8):
-        zcopy(o, blocks.at[cls, za], blocks.at[cls, (za + 4 - o // 4) % 4]).wait_recv()
-    for o in (1, 15, 2, 14):
-        wait_ready(o)
-        src = {1: blocks.at[cls], 15: blocks.at[cls], 2: blocks.at[cls, 0:2], 14: blocks.at[cls, 2:4]}[o]
-        copy = zcopy(o, src, src)
-        copy.start()
-        sent.append(copy)
-    other = (cls + 2) % 4
-    for o, got in (
-        (1, blocks.at[(cls + 3) % 4]), (15, blocks.at[(cls + 1) % 4]),
-        (2, blocks.at[other, 0:2]), (14, blocks.at[other, 2:4]),
-    ):
-        zcopy(o, got, got).wait_recv()
+    transform(1, 0, 0)
+    transform(1, 1, 0)
+    send(1, 0)
+
+    @pl.when(late)
+    def _():
+        forward()
+
+    transform(1, 0, 1)
+    transform(1, 1, 1)
+    send(1, 1)
+
+    @pl.when(z < 4)
+    def _():
+        spread()
+
+    @pl.when(z < 8)
+    def _():
+        forward()
+
+    for a in range(4):
+        near(1, a, (cls + 3) % 4).wait_recv()
+        near(15, a, (cls + 1) % 4).wait_recv()
+        near(2 if a < 2 else 14, a, (cls + 2) % 4).wait_recv()
 
     for r in range(REFS):
         zr, yr = r // 2, r % 2
@@ -260,41 +314,54 @@
         half = pl.ds(p * 32, 32)
         return pltpu.make_async_copy(out_ref.at[:, half], out_hbm.at[:, half], out_sem.at[p])
 
-    for p in range(2):
-        lax.fori_loop(p * 8, p * 8 + 8, build, 0)
+    def multiply(p, kg):
+        right = data[p, :, :, :, kg].reshape(512, CH)
+        both = jnp.dot(lhs[p * 8 + kg], right, preferred_element_type=jnp.float32) * scale
+        both = both.astype(jnp.bfloat16)
+        for b in range(4):
+            for ri in range(2):
+                out_ref[ri, (p * 8 + kg) * 4 + b] = both[(b * 2 + ri) * 32:(b * 2 + ri + 1) * 32]
+
+    def products(p, fused):
+        def step(n, _):
+            for j in range(4):
+                kg = n * 4 + j
+                if fused:
+                    build(p * 8 + kg, 0)
+                multiply(p, kg)
+            return 0
+
         for h in range(2):
-            own(h, p).wait()
-            for e in range(2):
-                for i in range(4):
-                    if not (e == 1 and i == 2):
-                        bulk_in(h, p, e, i).wait_recv()
-
-        def products(step, _):
-            for j in range(4):
-                kg = step * 4 + j
-                right = data[p, :, :, :, kg].reshape(512, CH)
-                both = jnp.dot(lhs[p * 8 + kg], right, preferred_element_type=jnp.float32) * scale
-                both = both.astype(jnp.bfloat16)
-                for b in range(4):
-                    for ri in range(2):
-                        out_ref[ri, (p * 8 + kg) * 4 + b] = both[(b * 2 + ri) * 32:(b * 2 + ri + 1) * 32]
-            return 0
-
-        lax.fori_loop(0, 2, products, 0)
+            receive(h, p)
+        lax.fori_loop(0, 2, step, 0)
         store_out(p).start()
+
+    @pl.when(z < 4)
+    def _():
+        products(0, True)
+        products(1, True)
+
+    @pl.when(z >= 4)
+    def _():
+        lax.fori_loop(0, 16, build, 0)
+        products(0, False)
+        products(1, False)
 
     cross[0].wait_send()
     cross[1].wait_send()
     for w, d in pairs:
         ref_copy(w, d, q).wait_send()
-    for copy in sent:
-        copy.wait_send()
+    for j in range(1, 4):
+        far(j, za).wait_send()
+    for a in range(4):
+        for o in (1, 15, 2 if a < 2 else 14):
+            near(o, a, cls).wait_send()
     for h in range(2):
         for p in range(2):
-            for e in range(2):
-                for i in range(4):
-                    if not (e == 1 and i == 2):
-                        bulk(h, p, e, i).wait_send()
+            for i in range(4):
+                over_y(h, p, i, q).wait_send()
+            for i in range(1, 4):
+                over_x(h, p, i, q).wait_send()
     store_out(0).wait()
     store_out(1).wait()
 
@@ -325,8 +392,9 @@
             pltpu.VMEM((4, 4, 2, 16, 512), bf16),
             pltpu.VMEM((4, REFS * 16, 128), f32),
             pltpu.VMEM((16, 256, 512), bf16),
-            dma, dma, dma((8,)), dma((2,)), dma((2,)), dma((2, 2, 8)), dma((2, 2, 8)), dma((2, 2)),
-            dma((2, 8)), dma((2, 8)), dma((7,)), dma((7,)), dma((2,)), pltpu.SemaphoreType.REGULAR((7,)),
+            dma, dma, dma((8,)), dma((2,)), dma((2,)), dma((2, 2)),
+            *[dma((2, 2, 4)) for _ in range(4)], dma((2, 8)), dma((2, 8)),
+            dma((4,)), dma((4,)), dma((4, 4)), dma((4, 4)), dma((2,)), pltpu.SemaphoreType.REGULAR((7,)),
         ],
         compiler_params=pltpu.CompilerParams(
             collective_id=0, has_side_effects=True, vmem_limit_bytes=52 * 2**20

time: 45.7 us -> 44.5 us (0.974)
  the two profiles are of different devices: /device:TPU:2 before, /device:TPU:6 now
where the time goes in v3:
time: 44.5 us; the launch traced here: 44.1 us
  Pallas kernels  42.4 us (95%)
  local copies, waits for them, and re-layouts  1.67 us (4%)
    pallas_call x1, Pallas kernels, local(): pl.pallas_call(kernel, out_shape=jax.ShapeDtypeStruct((2, 64, REFS, CH),...  42.4 us
    unnamed x3, local copies, waits for them, and re-layouts  1.67 us

profile of v3, /device:TPU:6, one launch (start us, length us, event | category | flops | bytes accessed | tf_op | source)
XLA Modules:
  0.0 44.1 jit_solution(2988414702604293763)
XLA Ops:
  0.0 0.0 copy-start
  0.0 0.7 %copy-done = f32[1,2048]{1,0:T(1,128)S(1)} copy-done((f32[1,2048]{1,0:T(1,128)S(1)}, f32[1,2048]{1,0:T(1,128)}, u32[]{:S(2)}) %copy-start) | copy-done | bytes 8216
  0.7 42.4 %cross_spectra.1 = bf16[2,64,32,128]{3,2,1,0:T(8,128)(2,1)S(1)} custom-call(bf16[128,8192]{1,0:T(8,128)(2,1)} %sig_hbm.1, bf16[2,8,2,64,2048]{4,3,2,1,0:T(8,128)(2,1)} %constant.4.clone.tab_hbm, f32[1,2048]{1,0:T(1,128)S(1)} %copy-done), custom_call_target="tpu_custom_call" | custom-call | flops 5000000000 | bytes 8000000 | tf_op jit(solution)/shard_map/cross_spectra/pallas_call | solution.py:372
  43.1 1.0 %copy.5 = bf16[2,64,32,128]{3,2,1,0:T(8,128)(2,1)} copy(bf16[2,64,32,128]{3,2,1,0:T(8,128)(2,1)S(1)} %cross_spectra.1) | data formatting | bytes 2097152
Async XLA Ops:
  0.0 0.7 %copy-start = (f32[1,2048]{1,0:T(1,128)S(1)}, f32[1,2048]{1,0:T(1,128)}, u32[]{:S(2)}) copy-start(f32[1,2048]{1,0:T(1,128)} %constant.5.clone.win_hbm) | copy-start | bytes 24580

commit v4 on v3

--- a/solution.py
+++ b/solution.py
@@ -324,8 +324,8 @@
 
     def products(p, fused):
         def step(n, _):
-            for j in range(4):
-                kg = n * 4 + j
+            for j in range(8):
+                kg = n * 8 + j
                 if fused:
                     build(p * 8 + kg, 0)
                 multiply(p, kg)
@@ -333,17 +333,22 @@
 
         for h in range(2):
             receive(h, p)
-        lax.fori_loop(0, 2, step, 0)
+        step(0, 0)
         store_out(p).start()
 
-    @pl.when(z < 4)
+    @pl.when(z < 8)
     def _():
         products(0, True)
         products(1, True)
 
-    @pl.when(z >= 4)
-    def _():
-        lax.fori_loop(0, 16, build, 0)
+    @pl.when(z >= 8)
+    def _():
+        def build_four(n, _):
+            for j in range(4):
+                build(n * 4 + j, 0)
+            return 0
+
+        lax.fori_loop(0, 4, build_four, 0)
         products(0, False)
         products(1, False)
 

time: 44.5 us -> 43.9 us (0.987)
  Pallas kernels: 42.4 us -> 41.8 us
    pallas_call x1, Pallas kernels: 42.4 us -> 41.8 us  [local(): pl.pallas_call(kernel, out_shape=jax.ShapeDtypeStruct((2, 64, REFS, CH),...]
where the time goes in v4:
time: 43.9 us; the launch traced here: 43.5 us
  Pallas kernels  41.8 us (95%)
  local copies, waits for them, and re-layouts  1.67 us (4%)
    pallas_call x1, Pallas kernels, local(): pl.pallas_call(kernel, out_shape=jax.ShapeDtypeStruct((2, 64, REFS, CH),...  41.8 us
    unnamed x3, local copies, waits for them, and re-layouts  1.67 us

profile of v4, /device:TPU:6, one launch (start us, length us, event | category | flops | bytes accessed | tf_op | source)
XLA Modules:
  0.0 43.5 jit_solution(18364694771962542438)
XLA Ops:
  0.0 0.0 copy-start
  0.0 0.7 %copy-done = f32[1,2048]{1,0:T(1,128)S(1)} copy-done((f32[1,2048]{1,0:T(1,128)S(1)}, f32[1,2048]{1,0:T(1,128)}, u32[]{:S(2)}) %copy-start) | copy-done | bytes 8216
  0.7 41.8 %cross_spectra.1 = bf16[2,64,32,128]{3,2,1,0:T(8,128)(2,1)S(1)} custom-call(bf16[128,8192]{1,0:T(8,128)(2,1)} %sig_hbm.1, bf16[2,8,2,64,2048]{4,3,2,1,0:T(8,128)(2,1)} %constant.4.clone.tab_hbm, f32[1,2048]{1,0:T(1,128)S(1)} %copy-done), custom_call_target="tpu_custom_call" | custom-call | flops 5000000000 | bytes 8000000 | tf_op jit(solution)/shard_map/cross_spectra/pallas_call | solution.py:377
  42.5 1.0 %copy.5 = bf16[2,64,32,128]{3,2,1,0:T(8,128)(2,1)} copy(bf16[2,64,32,128]{3,2,1,0:T(8,128)(2,1)S(1)} %cross_spectra.1) | data formatting | bytes 2097152
Async XLA Ops:
  0.0 0.7 %copy-start = (f32[1,2048]{1,0:T(1,128)S(1)}, f32[1,2048]{1,0:T(1,128)}, u32[]{:S(2)}) copy-start(f32[1,2048]{1,0:T(1,128)} %constant.5.clone.win_hbm) | copy-start | bytes 24580
